TPU v7x, 128 devices: a whole 4x4x4 slice. The times are simulated.
128 devices in a mesh: dp: 8 (over z_lo, x), fsdp: 16 (over y, z_hi, core).
Axes of the slice: x: 4, y: 4, z: 4 (z_hi: 2, z_lo: 2; z = z_hi * 2 + z_lo), core: 2. Of those that a mesh axis runs over, the one named last changes fastest.
Arguments:
- queries: bfloat16 [65536, 2048], P(('dp', 'fsdp')), may hold values from -6 to 6
- keys: bfloat16 [65536, 2048], P(('dp', 'fsdp')), may hold values from -6 to 6
- values: bfloat16 [65536, 2048], P(('dp', 'fsdp')), may hold values from -6 to 6
- attn_out: bfloat16 [65536, 2048], P(('dp', 'fsdp')), may hold values from -24 to 24
- out_grad: bfloat16 [65536, 2048], P(('dp', 'fsdp')), may hold values from -6 to 6
- log_norm: float32 [65536, 16], P(('dp', 'fsdp')), may hold values from 4 to 7
- segment_ids: int32 [128, 4], P(('dp', 'fsdp')), may hold values from 0 to 3, as said below
- kept_tokens: int32 [128, 4], P(('dp', 'fsdp')), may hold values from 0 to 512, as said below
- out_weight: bfloat16 [2048, 2048], P('fsdp'), may hold values from -0.125 to 0.125
Outputs:
- query_grad: bfloat16 [65536, 2048], P(('dp', 'fsdp'))
- key_grad: bfloat16 [65536, 2048], P(('dp', 'fsdp'))
- value_grad: bfloat16 [65536, 2048], P(('dp', 'fsdp'))
- weight_grad: float32 [2048, 2048], P('fsdp')
Inputs may be any that keep to these rules, and one draw needn't show every extreme that they name: `segment_ids`: row p numbers the images of pack p block by block: 0 for block 0, rising by one at each block that starts a new image. Some pack is one image, some pack has one image a block. `kept_tokens`: entry (p, i) counts the kept tokens of image i of pack p, which fill the start of that image's blocks: an image of b blocks keeps 128 (b - 1) + 1 to 128 b tokens; numbers with no image hold 0.
All inputs are finite; a program needn't handle non-finite values.
Results may differ from a plain program's by a relative error of at most 0.012.
The roundings to bfloat16 on the way count: a program that leaves them out, or rounds other values in their place, can miss the bound.
Values may be sent and summed in bfloat16 or wider, within the bound.
A program may use at most 192 MiB of HBM per device.

v0:
```python
import jax
import jax.numpy as jnp
from jax import lax
from jax.sharding import PartitionSpec as P

BLOCK = 128


def pair_grads(query_heads, key_heads, value_heads, grad_heads, norm_rows, delta_rows, key_live):
    score_scale = query_heads.shape[2] ** (-0.5)
    scores = (
        jnp.einsum("hqd,hkd->hqk", query_heads, key_heads, preferred_element_type=jnp.float32)
        * score_scale
    )
    probs = jnp.where(key_live[None, None, :], jnp.exp(scores - norm_rows[:, :, None]), 0.0)
    value_grad = jnp.einsum(
        "hqk,hqd->hkd", probs.astype(jnp.bfloat16), grad_heads, preferred_element_type=jnp.float32
    )
    prob_grad = jnp.einsum(
        "hqd,hkd->hqk", grad_heads, value_heads, preferred_element_type=jnp.float32
    )
    score_grad = (probs * (prob_grad - delta_rows[:, :, None])).astype(jnp.bfloat16)
    query_grad = (
        jnp.einsum("hqk,hkd->hqd", score_grad, key_heads, preferred_element_type=jnp.float32)
        * score_scale
    )
    key_grad = (
        jnp.einsum("hqk,hqd->hkd", score_grad, query_heads, preferred_element_type=jnp.float32)
        * score_scale
    )
    return (query_grad, key_grad, value_grad)


def to_blocks(rows, block_count, head_count):
    return rows.reshape(block_count, BLOCK, head_count, rows.shape[1] // head_count).transpose(
        0, 2, 1, 3
    )


def from_blocks(blocked):
    block_count, head_count, block_rows, head_size = blocked.shape
    return (
        blocked.transpose(0, 2, 1, 3)
        .reshape(block_count * block_rows, head_count * head_size)
        .astype(jnp.bfloat16)
    )


def per_device(
    queries, keys, values, attn_out, out_grad, log_norm, segment_ids, kept_tokens, out_weight
):
    tok_rows = queries.shape[0]
    feat_width = queries.shape[1]
    head_count = log_norm.shape[1]
    head_size = feat_width // head_count
    block_count = tok_rows // BLOCK
    seg_ids = segment_ids[0]
    kept_counts = kept_tokens[0]
    block_ids = jnp.arange(block_count)
    first_block = jnp.sum((seg_ids[None, :] < seg_ids[:, None]).astype(jnp.int32), axis=1)
    block_kept = jnp.sum(
        (seg_ids[:, None] == block_ids[None, :]).astype(jnp.int32) * kept_counts[None, :], axis=1
    )
    positions = (block_ids - first_block)[:, None] * BLOCK + jnp.arange(BLOCK)[None, :]
    block_valid = positions < block_kept[:, None]
    token_valid = block_valid.reshape(tok_rows)
    grad_input = jnp.where(token_valid[:, None], out_grad, jnp.zeros_like(out_grad))
    attn_grad = lax.dot_general(
        grad_input,
        lax.all_gather(out_weight, "fsdp", axis=0, tiled=True),
        (((1,), (1,)), ((), ())),
        preferred_element_type=jnp.float32,
    ).astype(jnp.bfloat16)
    delta = jnp.sum(
        (attn_grad.astype(jnp.float32) * attn_out.astype(jnp.float32)).reshape(
            tok_rows, head_count, head_size
        ),
        axis=2,
    )
    grad_share = lax.psum_scatter(
        lax.dot_general(
            attn_out, grad_input, (((0,), (0,)), ((), ())), preferred_element_type=jnp.float32
        ),
        "fsdp",
        scatter_dimension=0,
        tiled=True,
    )
    weight_grad = lax.psum(grad_share, "dp")
    query_blocks = to_blocks(queries, block_count, head_count)
    key_blocks = to_blocks(keys, block_count, head_count)
    value_blocks = to_blocks(values, block_count, head_count)
    grad_blocks = to_blocks(attn_grad, block_count, head_count)
    norm_blocks = log_norm.reshape(block_count, BLOCK, head_count).transpose(0, 2, 1)
    delta_blocks = delta.reshape(block_count, BLOCK, head_count).transpose(0, 2, 1)
    pair_ids = jnp.arange(block_count * block_count)
    pair_live = (seg_ids[pair_ids // block_count] == seg_ids[pair_ids % block_count]).astype(
        jnp.int32
    )
    pair_order = jnp.argsort(1 - pair_live, stable=True)
    pair_total = jnp.sum(pair_live)

    def take_blocks(query_block, key_block):
        return (
            query_blocks[query_block],
            key_blocks[key_block],
            value_blocks[key_block],
            grad_blocks[query_block],
            norm_blocks[query_block],
            delta_blocks[query_block],
            block_valid[key_block],
        )

    def run_pair(pair_step, totals):
        pair_index = pair_order[pair_step]
        query_block = pair_index // block_count
        key_block = pair_index % block_count
        query_term, key_term, value_term = pair_grads(*take_blocks(query_block, key_block))
        return (
            totals[0].at[query_block].add(query_term),
            totals[1].at[key_block].add(key_term),
            totals[2].at[key_block].add(value_term),
        )

    empty = jnp.zeros((block_count, head_count, BLOCK, head_size), jnp.float32)
    totals = (empty, empty, empty)
    totals = lax.fori_loop(0, pair_total, run_pair, totals)
    return (from_blocks(totals[0]), from_blocks(totals[1]), from_blocks(totals[2]), weight_grad)


def solution(mesh):
    placed = (
        P(("dp", "fsdp"), None),
        P(("dp", "fsdp"), None),
        P(("dp", "fsdp"), None),
        P(("dp", "fsdp"), None),
        P(("dp", "fsdp"), None),
        P(("dp", "fsdp"), None),
        P(("dp", "fsdp"), None),
        P(("dp", "fsdp"), None),
        P("fsdp", None),
    )
    return jax.shard_map(
        per_device,
        mesh=mesh,
        in_specs=placed,
        out_specs=(
            P(("dp", "fsdp"), None),
            P(("dp", "fsdp"), None),
            P(("dp", "fsdp"), None),
            P("fsdp", None),
        ),
        check_vma=False,
    )
```

profile of v0, /device:TPU:0, one launch (start us, length us, event | category | flops | bytes accessed | tf_op | source)
XLA Modules:
  0.0 482.5 jit_solution(11948150179926760325)
XLA Ops:
  9.0 12.6 %convolution_bitcast_fusion.1 = f32[2048,2048]{0,1:T(8,128)} fusion(bf16[512,2048]{1,0:T(8,128)(2,1)} %param.20, bf16[512,2048]{1,0:T(8,128)(2,1)} %param.21, pred[512]{0:T(512)(128)(4,1)S(1)} %fusion.27), kind=kOutput, calls=%fused_computation.45 | convolution fusion | flops 4296015872 | bytes 20972032 | tf_op jit(solution)/shard_map/dot_general | solution.py:81
  37.7 48.0 %all-gather.2.cloned.1.call-done = bf16[2048,2048]{1,0:T(8,128)(2,1)} async-done(((bf16[128,2048]{1,0:T(8,128)(2,1)}), bf16[2048,2048]{1,0:T(8,128)(2,1)}) %all-gather.2.cloned.1.call-update) | async-done | bytes 8388624 | tf_op jit(solution)/shard_map/all_gather | solution.py:70
  85.7 8.4 %convolution_convert_fusion = bf16[512,2048]{1,0:T(8,128)(2,1)S(1)} fusion(bf16[2048,2048]{1,0:T(8,128)(2,1)} %all-gather.2.cloned.1.call-done, bf16[512,2048]{1,0:T(8,128)(2,1)S(1)} %copy-done.10, pred[512]{0:T(512)(128)(4,1)S(1)} %fusion.27), kind=kOutput, calls=%fused_computation.47 | convolution fusion | flops 4297064448 | bytes 12583424 | tf_op jit(solution)/shard_map/dot_general | solution.py:68
  100.6 4.1 reduce_sum.39
  113.1 286.7 %while.19 = (s32[]{:T(128)}, f32[4,16,128,128]{3,2,1,0:T(8,128)}, f32[4,16,128,128]{3,2,1,0:T(8,128)}, f32[4,16,128,128]{3,2,1,0:T(8,128)}, s32[]{:T(128)}, /*in...) while((s32[]{:T(128)}, f32[4,16,128,128]{3,2,1,0:T(8,128)}, ...), condition=%wide.region_8.9_spmd, body=%wide.region_5.8_spmd.sunk | while | flops 339476544 | bytes 17879468 | solution.py:126
  121.6 3.3 fusion.49
  128.1 3.5 fusion.48
  146.2 3.3 fusion.48
  157.7 3.2 fusion.49
  164.2 3.2 fusion.48
  193.4 3.3 fusion.49
  196.7 3.3 fusion.47
  214.7 3.3 fusion.47
  217.9 3.3 fusion.48
  232.6 3.2 fusion.47
  235.8 3.2 fusion.48
  250.4 3.2 fusion.47
  265.0 3.3 fusion.49
  289.3 3.2 fusion.48
  307.1 3.2 fusion.48
  336.2 3.3 fusion.49
  360.5 3.2 fusion.48
  378.3 3.2 fusion.48
  415.2 58.2 %all-reduce.2.cloned.1.call-done = f32[128,2048]{0,1:T(8,128)} async-done(((f32[128,2048]{0,1:T(8,128)}), f32[128,2048]{0,1:T(8,128)}) %all-reduce.2.cloned.1.call-update) | async-done | bytes 1048592 | tf_op jit(solution)/shard_map/psum | solution.py:88
  (224 shorter events, 225.3 us)
Async XLA Ops:
  7.2 78.5 %all-gather.2.cloned.1.call-start = ((), (), s32[]{:S(2)}) async-start(), calls=%async_computation.1 | async-start | bytes 8912896 | tf_op jit(solution)/shard_map/all_gather | solution.py:70
  7.9 392.0 %reduce-scatter.2.cloned.1.call-start = ((), (), s32[]{:S(2)}) async-start(), calls=%async_computation.2 | async-start | bytes 17825792 | tf_op jit(solution)/shard_map/reduce_scatter | solution.py:80
  21.6 0.7 copy-start
  21.6 2.0 copy-start.8
  21.6 451.8 %all-reduce.2.cloned.1.call-start = ((), (), s32[]{:S(2)}) async-start(), calls=%async_computation.3 | async-start | bytes 2097152 | tf_op jit(solution)/shard_map/psum | solution.py:88
  23.6 2.4 copy-start.5
  26.0 2.0 copy-start.6
  31.9 2.2 copy-start.3
  31.9 3.0 copy-start.4
  35.0 50.8 %copy-start.10 = (bf16[512,2048]{1,0:T(8,128)(2,1)S(1)}, bf16[512,2048]{1,0:T(8,128)(2,1)}, u32[]{:S(2)}) copy-start(bf16[512,2048]{1,0:T(8,128)(2,1)} %param.21) | copy-start | bytes 6291460
  94.7 2.0 copy-start.7
  110.4 2.8 copy-start.9
  403.9 3.0 copy-start.2
  408.6 3.0 copy-start.1
Sparse Core Ops, SparseCore 0:
  10.4 75.2 all-gather.1
  90.1 145.1 reduce-scatter.1
  400.1 73.3 all-reduce.1
where the time goes:
time: 487 us; the launch traced here: 482 us
  matrix products  192 us (39%)
  waiting for transfers between devices  107 us (22%)
  local copies, waits for them, and re-layouts  92.4 us (19%)
  loops' own time  53.1 us (11%)
  other arithmetic  23.7 us (5%)
  between operations  14 us (3%)
    psum x1, waiting for transfers between devices, per_device(): weight_grad = lax.psum(grad_share, 'dp')  58.2 us
    another operation x1, loops' own time, per_device(): totals = lax.fori_loop(0, pair_total, run_pair, totals)  53.1 us
    dot_general x16, matrix products, pair_grads(): jnp.einsum('hqk,hqd->hkd', score_grad, query_heads, preferred_element_typ...  51.7 us
    dot_general x16, matrix products, pair_grads(): jnp.einsum('hqk,hqd->hkd', probs.astype(jnp.bfloat16), grad_heads, prefer...  51.5 us
    dot_general x16, matrix products, pair_grads(): jnp.einsum('hqk,hkd->hqd', score_grad, key_heads, preferred_element_type=...  51.3 us
    all_gather x1, waiting for transfers between devices, per_device(): lax.all_gather(out_weight, 'fsdp', axis=0, tiled=True)  48 us
    unnamed x31, local copies, waits for them, and re-layouts  23.6 us
    dynamic_slice x16, local copies, waits for them, and re-layouts, take_blocks(): value_blocks[key_block]  22.3 us
  transfers between devices with their start and end apart: 3, of which 2 were waited for; matrix products, arithmetic and copies ran while one was open for 62% of the time, Pallas kernels for 0%

commit v1 on v0

--- a/solution.py
+++ b/solution.py
@@ -4,6 +4,12 @@
 from jax.sharding import PartitionSpec as P
 
 BLOCK = 128
+
+
+def summed_here(x, mesh_axis):
+    terms = lax.all_gather(x, mesh_axis, axis=0, tiled=False)
+    total = terms.sum(axis=0)
+    return total
 
 
 def pair_grads(query_heads, key_heads, value_heads, grad_heads, norm_rows, delta_rows, key_live):
@@ -85,7 +91,7 @@
         scatter_dimension=0,
         tiled=True,
     )
-    weight_grad = lax.psum(grad_share, "dp")
+    weight_grad = summed_here(grad_share, "dp")
     query_blocks = to_blocks(queries, block_count, head_count)
     key_blocks = to_blocks(keys, block_count, head_count)
     value_blocks = to_blocks(values, block_count, head_count)

time: 487 us -> 599 us (1.23)
  waiting for transfers between devices: 107 us -> 207 us
  other arithmetic: 23.7 us -> 34.7 us
    reduce_scatter x1, waiting for transfers between devices: 0.02 us -> 149 us  [per_device(): lax.psum_scatter(lax.dot_general(attn_out, grad_input, (((0,), (0,)), (()...]
    psum x1 -> x0, waiting for transfers between devices: 58.2 us -> none  [per_device(): weight_grad = lax.psum(grad_share, 'dp')]
    reduce_sum x0 -> x1, other arithmetic: none -> 11.6 us  [summed_here(): total = terms.sum(axis=0)]
    all_gather x1, waiting for transfers between devices: 48 us -> 57.5 us  [per_device(): lax.all_gather(out_weight, 'fsdp', axis=0, tiled=True)]
    unnamed x31 -> x32, local copies, waits for them, and re-layouts: 23.6 us -> 26.8 us
  transfers between devices with their start and end apart: 3 -> 3, of which waited for: 2 -> 2; matrix products, arithmetic and copies ran while one was open for 62% -> 48% of each run, Pallas kernels for 0% -> 0%
where the time goes in v1:
time: 599 us; the launch traced here: 594 us
  waiting for transfers between devices  207 us (35%)
  matrix products  191 us (32%)
  local copies, waits for them, and re-layouts  94.2 us (16%)
  loops' own time  52.7 us (9%)
  other arithmetic  34.7 us (6%)
  between operations  14 us (2%)
    reduce_scatter x1, waiting for transfers between devices, per_device(): lax.psum_scatter(lax.dot_general(attn_out, grad_input, (((0,), (0,)), (()...  149 us
    all_gather x1, waiting for transfers between devices, per_device(): lax.all_gather(out_weight, 'fsdp', axis=0, tiled=True)  57.5 us
    another operation x1, loops' own time, per_device(): totals = lax.fori_loop(0, pair_total, run_pair, totals)  52.7 us
    dot_general x16, matrix products, pair_grads(): jnp.einsum('hqk,hkd->hqd', score_grad, key_heads, preferred_element_type=...  51.3 us
    dot_general x16, matrix products, pair_grads(): jnp.einsum('hqk,hqd->hkd', probs.astype(jnp.bfloat16), grad_heads, prefer...  51.2 us
    dot_general x16, matrix products, pair_grads(): jnp.einsum('hqk,hqd->hkd', score_grad, query_heads, preferred_element_typ...  51.2 us
    unnamed x32, local copies, waits for them, and re-layouts  26.8 us
    dynamic_slice x16, local copies, waits for them, and re-layouts, take_blocks(): value_blocks[key_block]  22.2 us
  transfers between devices with their start and end apart: 3, of which 2 were waited for; matrix products, arithmetic and copies ran while one was open for 48% of the time, Pallas kernels for 0%

profile of v1, /device:TPU:0, one launch (start us, length us, event | category | flops | bytes accessed | tf_op | source)
XLA Modules:
  0.0 594.0 jit_solution(10618699884986375182)
XLA Ops:
  8.2 12.6 %convolution_bitcast_fusion.1 = f32[2048,2048]{0,1:T(8,128)} fusion(bf16[512,2048]{1,0:T(8,128)(2,1)} %param.20, bf16[512,2048]{1,0:T(8,128)(2,1)} %param.21, pred[512]{0:T(512)(128)(4,1)S(1)} %fusion.27), kind=kOutput, calls=%fused_computation.45 | convolution fusion | flops 4296015872 | bytes 20972032 | tf_op jit(solution)/shard_map/dot_general | solution.py:87
  21.9 148.8 %reduce-scatter.2.cloned.1.call-done = f32[128,2048]{0,1:T(8,128)} async-done(((f32[2048,2048]{0,1:T(8,128)}), f32[128,2048]{0,1:T(8,128)}) %reduce-scatter.2.cloned.1.call-update) | async-done | bytes 1048592 | tf_op jit(solution)/shard_map/reduce_scatter | solution.py:86
  186.3 57.5 %all-gather.4.cloned.1.call-done = bf16[2048,2048]{1,0:T(8,128)(2,1)} async-done(((bf16[128,2048]{1,0:T(8,128)(2,1)}), bf16[2048,2048]{1,0:T(8,128)(2,1)}) %all-gather.4.cloned.1.call-update) | async-done | bytes 8388624 | tf_op jit(solution)/shard_map/all_gather | solution.py:76
  243.8 8.3 %convolution_convert_fusion = bf16[512,2048]{1,0:T(8,128)(2,1)S(1)} fusion(bf16[2048,2048]{1,0:T(8,128)(2,1)} %all-gather.4.cloned.1.call-done, bf16[512,2048]{1,0:T(8,128)(2,1)S(1)} %copy-done.10, pred[512]{0:T(512)(128)(4,1)S(1)} %fusion.27), kind=kOutput, calls=%fused_computation.48 | convolution fusion | flops 4297064448 | bytes 12583424 | tf_op jit(solution)/shard_map/dot_general | solution.py:74
  258.1 3.4 reduce_sum.48
  268.9 285.0 %while.19 = (s32[]{:T(128)}, f32[4,16,128,128]{3,2,1,0:T(8,128)}, f32[4,16,128,128]{3,2,1,0:T(8,128)}, f32[4,16,128,128]{3,2,1,0:T(8,128)}, s32[]{:T(128)}, /*in...) while((s32[]{:T(128)}, f32[4,16,128,128]{3,2,1,0:T(8,128)}, ...), condition=%wide.region_8.9_spmd, body=%wide.region_5.8_spmd.sunk | while | flops 339476544 | bytes 17879468 | solution.py:132
  277.3 3.2 fusion.49
  280.5 3.3 fusion.47
  283.8 3.3 fusion.48
  295.2 3.3 fusion.49
  298.5 3.3 fusion.47
  316.3 3.3 fusion.47
  319.5 3.2 fusion.48
  330.9 3.2 fusion.49
  334.1 3.3 fusion.47
  337.4 3.2 fusion.48
  355.1 3.2 fusion.48
  366.5 3.2 fusion.49
  426.0 3.2 fusion.48
  437.4 3.2 fusion.49
  496.9 3.2 fusion.48
  508.3 3.2 fusion.49
  569.1 5.5 copy.72
  574.6 11.6 %bitcast_reduce_fusion = f32[128,2048]{0,1:T(8,128)S(1)} fusion(f32[256,8,8,128]{3,2,1,0:T(8,128)S(1)} %copy.72), kind=kLoop, calls=%fused_computation.46 | loop fusion | flops 1835008 | bytes 9437184 | tf_op jit(solution)/shard_map/reduce_sum | solution.py:11
  (226 shorter events, 227.7 us)
Async XLA Ops:
  7.2 163.5 %reduce-scatter.2.cloned.1.call-start = ((), (), s32[]{:S(2)}) async-start(), calls=%async_computation.2 | async-start | bytes 17825792 | tf_op jit(solution)/shard_map/reduce_scatter | solution.py:86
  20.9 149.8 %copy-start = (s32[1,4]{1,0:T(1,128)S(1)}, s32[1,4]{1,0:T(1,128)}, u32[]{:S(2)}) copy-start(s32[1,4]{1,0:T(1,128)} %param.23) | copy-start | bytes 52
  20.9 151.2 %copy-start.8 = (f32[512,16]{0,1:T(8,128)S(1)}, f32[512,16]{0,1:T(8,128)}, u32[]{:S(2)}) copy-start(f32[512,16]{0,1:T(8,128)} %param.22) | copy-start | bytes 98308
  20.9 222.9 %all-gather.4.cloned.1.call-start = ((), (), s32[]{:S(2)}) async-start(), calls=%async_computation.1 | async-start | bytes 8912896 | tf_op jit(solution)/shard_map/all_gather | solution.py:76
  21.6 547.4 %all-gather.6.cloned.1.call-start = ((), (), s32[]{:S(2)}) async-start(), calls=%async_computation.3 | async-start | bytes 9437184 | tf_op jit(solution)/shard_map/all_gather | solution.py:10
  172.1 2.4 copy-start.5
  174.4 2.0 copy-start.6
  180.4 2.5 copy-start.3
  180.4 3.2 copy-start.4
  183.6 60.3 %copy-start.10 = (bf16[512,2048]{1,0:T(8,128)(2,1)S(1)}, bf16[512,2048]{1,0:T(8,128)(2,1)}, u32[]{:S(2)}) copy-start(bf16[512,2048]{1,0:T(8,128)(2,1)} %param.21) | copy-start | bytes 6291460
  252.8 1.6 copy-start.7
  266.5 2.5 copy-start.9
  557.9 2.9 copy-start.2
  562.5 2.9 copy-start.1
Sparse Core Ops, SparseCore 0:
  21.0 149.5 reduce-scatter.1
  173.3 70.4 all-gather.3
  245.5 95.6 all-gather.5
